TPU v7x, 32 devices: a whole 2x2x4 slice. The times are simulated.
32 devices in a mesh: rows: 16 (over z, y, core), cols: 2 (over x).
Axes of the slice: x: 2, y: 2, z: 4, core: 2. Of those that a mesh axis runs over, the one named last changes fastest.
Arguments:
- lower_coupling: bfloat16 [16, 1024, 1024], P('rows', 'cols'), may hold values from -0.0625 to 0.0625
- upper_coupling: bfloat16 [16, 1024, 1024], P('rows', 'cols'), may hold values from -0.0625 to 0.0625
- solution: bfloat16 [16, 1024, 256], P('rows', None, 'cols'), may hold values from -0.375 to 0.375
- cotangent: bfloat16 [16, 1024, 256], P('rows', None, 'cols'), may hold values from -6 to 6
Outputs:
- source_grad: bfloat16 [16, 1024, 256], P('rows', None, 'cols')
- lower_grad: bfloat16 [16, 1024, 1024], P('rows', 'cols')
- upper_grad: bfloat16 [16, 1024, 1024], P('rows', 'cols')
All inputs are finite; a program needn't handle non-finite values.
Results may differ from a plain program's by a relative error of at most 0.0085.
Values may be sent and summed in bfloat16 or wider, within the bound.
A program may use at most 64 MiB of HBM per device.

v0:
```python
import jax
import jax.numpy as jnp
from jax import lax
from jax.sharding import PartitionSpec as P


def shifted(value, axis, steps):
    count = lax.axis_size(axis)
    pairs = [(source, (source + steps) % count) for source in range(count)]
    return lax.ppermute(value, axis, pairs)


def make_pushes(picked, adjoint, lower_full, upper_full):

    def compute(operands):
        state, lower_mat, upper_mat = operands
        factor = state.astype(jnp.bfloat16)
        contract = (((0,), (0,)), ((), ()))
        push_down = lax.dot_general(lower_mat, factor, contract, preferred_element_type=jnp.float32)
        push_up = lax.dot_general(upper_mat, factor, contract, preferred_element_type=jnp.float32)
        return (push_down.astype(jnp.bfloat16), push_up.astype(jnp.bfloat16))

    def silent(operands):
        state = operands[0]
        blank = jnp.zeros(state.shape, jnp.bfloat16)
        return (blank, blank)

    return lax.cond(picked, compute, silent, (adjoint, lower_full, upper_full))


def body(lower_coupling, upper_coupling, solution, cotangent):
    row_count = lax.axis_size("rows")
    position = lax.axis_index("rows")
    offset = (position - 1) % row_count
    levels = row_count.bit_length() - 1
    lower_all, upper_all = (
        lax.all_gather(lower_coupling, "cols", axis=1, tiled=True),
        lax.all_gather(upper_coupling, "cols", axis=1, tiled=True),
    )
    lower_full = lower_all[0]
    upper_full = upper_all[0]
    own_block = solution[0]
    adjoint = cotangent[0].astype(jnp.float32)
    block_below = jnp.zeros_like(own_block)
    block_above = jnp.zeros_like(own_block)
    for level_no in range(levels):
        stride = 1 << level_no
        picked = offset % (2 * stride) == stride
        got_below = shifted(own_block, "rows", stride)
        got_above = shifted(own_block, "rows", -stride)
        block_below = jnp.where(picked, got_below, block_below)
        block_above = jnp.where(picked, got_above, block_above)
    for level_no in range(levels):
        stride = 1 << level_no
        picked = offset % (2 * stride) == stride
        push_down, push_up = make_pushes(picked, adjoint, lower_full, upper_full)
        from_below = shifted(push_up, "rows", stride)
        from_above = shifted(push_down, "rows", -stride)
        adjoint = adjoint - from_below.astype(jnp.float32) - from_above.astype(jnp.float32)
    factor = adjoint.astype(jnp.bfloat16)
    half_rows = lax.all_to_all(factor, "cols", split_axis=0, concat_axis=1, tiled=True)
    neighbours = lax.all_gather(jnp.stack((block_below, block_above)), "cols", axis=2, tiled=True)
    contract = (((1,), (1,)), ((), ()))
    grad_low = -lax.dot_general(
        half_rows, neighbours[0], contract, preferred_element_type=jnp.float32
    )
    grad_high = -lax.dot_general(
        half_rows, neighbours[1], contract, preferred_element_type=jnp.float32
    )
    return (factor[None], grad_low.astype(jnp.bfloat16)[None], grad_high.astype(jnp.bfloat16)[None])


def solution(mesh):
    in_specs = (
        P("rows", "cols", None),
        P("rows", "cols", None),
        P("rows", None, "cols"),
        P("rows", None, "cols"),
    )
    out_specs = (P("rows", None, "cols"), P("rows", "cols", None), P("rows", "cols", None))
    return jax.shard_map(body, mesh=mesh, in_specs=in_specs, out_specs=out_specs, check_vma=False)
```

profile of v0, /device:TPU:1, one launch (start us, length us, event | category | flops | bytes accessed | tf_op | source)
XLA Modules:
  0.0 199.7 jit_solution(3525152759680283863)
XLA Ops:
  7.2 0.0 copy-start.4
  7.2 0.0 all-gather.4.cloned.1.call-start
  7.2 0.7 all-gather.4.cloned.1.call-update
  7.9 0.0 all-gather.6.cloned.1.call-start
  8.0 0.7 all-gather.6.cloned.1.call-update
  8.7 0.0 all-gather.8.cloned.1.call-start
  8.7 36.0 %all-gather.4.cloned.1.call-done = bf16[1,1024,1024]{2,1,0:T(8,128)(2,1)} async-done(((bf16[1,512,1024]{2,1,0:T(8,128)(2,1)}), bf16[1,1024,1024]{2,1,0:T(8,128)(2,1)}) %all-gather.4.cloned.1.call-update) | async-done | bytes 2097168 | tf_op jit(solution)/shard_map/all_gather | solution.py:37
  44.8 34.7 %all-gather.6.cloned.1.call-done = bf16[1,1024,1024]{2,1,0:T(8,128)(2,1)} async-done(((bf16[1,512,1024]{2,1,0:T(8,128)(2,1)}), bf16[1,1024,1024]{2,1,0:T(8,128)(2,1)}) %all-gather.6.cloned.1.call-update) | async-done | bytes 2097168 | tf_op jit(solution)/shard_map/all_gather | solution.py:38
  79.5 0.0 copy-done.4
  79.5 0.1 conditional.4
  79.6 5.0 %collective-permute-start = (bf16[1024,128]{1,0:T(8,128)(2,1)S(1)}, bf16[1024,128]{1,0:T(8,128)(2,1)S(1)}, u32[]{:S(2)}, u32[]{:S(2)}) collective-permute-start(bf16[1024,128]{1,0:T(8,128)(2,1)S(1)} %get-tuple-element.47), channel_id=1, source_target_pairs={{0,2},{2,4},{4,6},{6,8},{8,10},{10,12},{12,14},{14,16},{16,18},{18... | collective-permute-start | bytes 786440 | tf_op jit(solution)/shard_map/ppermute | solution.py:10
  84.6 0.0 collective-permute-start.1
  84.6 1.2 collective-permute-start.10
  85.8 2.9 %collective-permute-start.11 = (bf16[1024,128]{1,0:T(8,128)(2,1)}, bf16[1024,128]{1,0:T(8,128)(2,1)S(1)}, u32[]{:S(2)}, u32[]{:S(2)}) collective-permute-start(bf16[1024,128]{1,0:T(8,128)(2,1)} %bitcast.8), channel_id=1, source_target_pairs={{0,2},{2,4},{4,6},{6,8},{8,10},{10,12},{12,14},{14,16},{16,18},{18... | collective-permute-start | bytes 786440 | tf_op jit(solution)/shard_map/ppermute | solution.py:10
  88.7 0.0 collective-permute-done
  88.7 12.9 %collective-permute-done.1 = bf16[1024,128]{1,0:T(8,128)(2,1)S(1)} collective-permute-done((bf16[1024,128]{1,0:T(8,128)(2,1)S(1)}, bf16[1024,128]{1,0:T(8,128)(2,1)S(1)}, u32[]{:S(2)}, u32[]{:S(2)}) %collective-permute-start.1) | collective-permute-done | bytes 262176 | tf_op jit(solution)/shard_map/ppermute | solution.py:10
  101.6 0.1 convert_subtract_fusion.2
  101.7 0.1 conditional.5
  101.8 0.1 collective-permute-start.2
  101.9 4.1 %collective-permute-start.3 = (bf16[1024,128]{1,0:T(8,128)(2,1)S(1)}, bf16[1024,128]{1,0:T(8,128)(2,1)S(1)}, u32[]{:S(2)}, u32[]{:S(2)}) collective-permute-start(bf16[1024,128]{1,0:T(8,128)(2,1)S(1)} %get-tuple-element.50), channel_id=1, source_target_pairs={{0,28},{2,30},{4,0},{6,2},{8,4},{10,6},{12,8},{14,10},{16,12},{18,... | collective-permute-start | bytes 786440 | tf_op jit(solution)/shard_map/ppermute | solution.py:10
  106.0 0.4 collective-permute-start.12
  106.4 0.0 collective-permute-done.10
  106.4 0.0 collective-permute-start.13
  106.4 0.0 collective-permute-done.11
  106.4 0.1 collective-permute-start.14
  106.6 6.7 %collective-permute-done.2 = bf16[1024,128]{1,0:T(8,128)(2,1)S(1)} collective-permute-done((bf16[1024,128]{1,0:T(8,128)(2,1)S(1)}, bf16[1024,128]{1,0:T(8,128)(2,1)S(1)}, u32[]{:S(2)}, u32[]{:S(2)}) %collective-permute-start.2) | collective-permute-done | bytes 262176 | tf_op jit(solution)/shard_map/ppermute | solution.py:10
  113.3 1.3 collective-permute-start.8
  114.5 0.8 collective-permute-done.3
  115.3 0.5 collective-permute-start.9
  115.8 0.1 convert_subtract_fusion.1
  115.9 0.1 conditional.6
  116.0 2.0 %collective-permute-done.12 = bf16[1024,128]{1,0:T(8,128)(2,1)} collective-permute-done((bf16[1024,128]{1,0:T(8,128)(2,1)}, bf16[1024,128]{1,0:T(8,128)(2,1)}, u32[]{:S(2)}, u32[]{:S(2)}) %collective-permute-start.12) | collective-permute-done | bytes 262176 | tf_op jit(solution)/shard_map/ppermute | solution.py:10
  118.0 1.5 collective-permute-start.4
  119.6 4.1 %collective-permute-done.13 = bf16[1024,128]{1,0:T(8,128)(2,1)} collective-permute-done((bf16[1024,128]{1,0:T(8,128)(2,1)}, bf16[1024,128]{1,0:T(8,128)(2,1)}, u32[]{:S(2)}, u32[]{:S(2)}) %collective-permute-start.13) | collective-permute-done | bytes 262176 | tf_op jit(solution)/shard_map/ppermute | solution.py:10
  123.7 0.2 collective-permute-start.5
  123.9 0.2 collective-permute-done.14
  124.1 22.0 %collective-permute-done.8 = bf16[1024,128]{1,0:T(8,128)(2,1)S(1)} collective-permute-done((bf16[1024,128]{1,0:T(8,128)(2,1)}, bf16[1024,128]{1,0:T(8,128)(2,1)S(1)}, u32[]{:S(2)}, u32[]{:S(2)}) %collective-permute-start.8) | collective-permute-done | bytes 262176 | tf_op jit(solution)/shard_map/ppermute | solution.py:10
  146.1 0.0 collective-permute-done.9
  146.1 0.1 select_bitcast_fusion.1
  146.2 0.0 copy-start
  146.2 0.8 pad_maximum_fusion
  147.1 0.0 all-gather.8.cloned.1.call-update
  147.1 0.0 collective-permute-done.4
  147.1 0.0 collective-permute-done.5
  147.1 1.0 convert_subtract_fusion
  148.1 0.0 copy-done
  148.1 0.1 conditional.7
  148.3 11.7 %collective-permute-start.6 = (bf16[1024,128]{1,0:T(8,128)(2,1)S(1)}, bf16[1024,128]{1,0:T(8,128)(2,1)S(1)}, u32[]{:S(2)}, u32[]{:S(2)}) collective-permute-start(bf16[1024,128]{1,0:T(8,128)(2,1)S(1)} %get-tuple-element.53), channel_id=1, source_target_pairs={{0,16},{2,18},{4,20},{6,22},{8,24},{10,26},{12,28},{14,30},{16,0},... | collective-permute-start | bytes 786440 | tf_op jit(solution)/shard_map/ppermute | solution.py:10
  159.9 0.1 collective-permute-start.7
  160.0 15.2 %collective-permute-done.6 = bf16[1024,128]{1,0:T(8,128)(2,1)S(1)} collective-permute-done((bf16[1024,128]{1,0:T(8,128)(2,1)S(1)}, bf16[1024,128]{1,0:T(8,128)(2,1)S(1)}, u32[]{:S(2)}, u32[]{:S(2)}) %collective-permute-start.6) | collective-permute-done | bytes 262176 | tf_op jit(solution)/shard_map/ppermute | solution.py:10
  175.2 5.4 %collective-permute-done.7 = bf16[1024,128]{1,0:T(8,128)(2,1)S(1)} collective-permute-done((bf16[1024,128]{1,0:T(8,128)(2,1)S(1)}, bf16[1024,128]{1,0:T(8,128)(2,1)S(1)}, u32[]{:S(2)}, u32[]{:S(2)}) %collective-permute-start.7) | collective-permute-done | bytes 262176 | tf_op jit(solution)/shard_map/ppermute | solution.py:10
  180.6 0.1 subtract_convert_fusion
  180.7 0.0 copy-start.5
  180.7 7.3 %all_to_all.19 = bf16[2,512,128]{2,1,0:T(8,128)(2,1)S(1)} all-to-all(bf16[2,512,128]{2,1,0:T(8,128)(2,1)S(1)} %bitcast.50), channel_id=1, replica_groups=mesh['rows'=16,'cols'=2] {'cols'}, dimensions={0} | all-to-all | bytes 524288 | tf_op jit(solution)/shard_map/all_to_all | solution.py:61
  188.0 0.1 copy.7
  188.2 0.0 all-gather.8.cloned.1.call-done
  188.2 2.5 %fusion.9 = bf16[1,512,1024]{2,1,0:T(8,128)(2,1)} fusion(bf16[512,256]{0,1:T(8,128)(2,1)S(1)} %bitcast.48, bf16[2,1024,256]{2,1,0:T(8,128)(2,1)} %all-gather.8.cloned.1.call-done), kind=kOutput, calls=%fused_computation.19 | convolution fusion | flops 269484032 | bytes 1835008 | tf_op jit(solution)/shard_map/dot_general | solution.py:67
  190.7 2.5 %fusion.8 = bf16[1,512,1024]{2,1,0:T(8,128)(2,1)} fusion(bf16[512,256]{0,1:T(8,128)(2,1)S(1)} %bitcast.49, bf16[2,1024,256]{2,1,0:T(8,128)(2,1)} %all-gather.8.cloned.1.call-done), kind=kOutput, calls=%fused_computation.18 | convolution fusion | flops 269484032 | bytes 1835008 | tf_op jit(solution)/shard_map/dot_general | solution.py:64
  193.2 0.0 copy-done.5
  (8 shorter events, 0.3 us)
Async XLA Ops:
  7.2 72.3 %copy-start.4 = (bf16[1,1024,128]{2,1,0:T(8,128)(2,1)S(1)}, bf16[1,1024,128]{2,1,0:T(8,128)(2,1)}, u32[]{:S(2)}) copy-start(bf16[1,1024,128]{2,1,0:T(8,128)(2,1)} %param.15) | copy-start | bytes 786436
  7.2 37.6 %all-gather.4.cloned.1.call-start = ((), (), s32[]{:S(2)}) async-start(), calls=%async_computation.1 | async-start | bytes 3145728 | tf_op jit(solution)/shard_map/all_gather | solution.py:37
  7.9 71.6 %all-gather.6.cloned.1.call-start = ((), (), s32[]{:S(2)}) async-start(), calls=%async_computation.2 | async-start | bytes 3145728 | tf_op jit(solution)/shard_map/all_gather | solution.py:38
  8.7 179.5 %all-gather.8.cloned.1.call-start = ((), (), s32[]{:S(2)}) async-start(), calls=%async_computation.3 | async-start | bytes 1572864 | tf_op jit(solution)/shard_map/all_gather | solution.py:62
  79.6 9.1 %collective-permute-start = (bf16[1024,128]{1,0:T(8,128)(2,1)S(1)}, bf16[1024,128]{1,0:T(8,128)(2,1)S(1)}, u32[]{:S(2)}, u32[]{:S(2)}) collective-permute-start(bf16[1024,128]{1,0:T(8,128)(2,1)S(1)} %get-tuple-element.47), channel_id=1, source_target_pairs={{0,2},{2,4},{4,6},{6,8},{8,10},{10,12},{12,14},{14,16},{16,18},{18... | collective-permute-start | bytes 786440 | tf_op jit(solution)/shard_map/ppermute | solution.py:10
  84.6 17.0 %collective-permute-start.1 = (bf16[1024,128]{1,0:T(8,128)(2,1)S(1)}, bf16[1024,128]{1,0:T(8,128)(2,1)S(1)}, u32[]{:S(2)}, u32[]{:S(2)}) collective-permute-start(bf16[1024,128]{1,0:T(8,128)(2,1)S(1)} %get-tuple-element.48), channel_id=1, source_target_pairs={{0,30},{2,0},{4,2},{6,4},{8,6},{10,8},{12,10},{14,12},{16,14},{18,... | collective-permute-start | bytes 786440 | tf_op jit(solution)/shard_map/ppermute | solution.py:10
  84.6 21.8 %collective-permute-start.10 = (bf16[1024,128]{1,0:T(8,128)(2,1)}, bf16[1024,128]{1,0:T(8,128)(2,1)S(1)}, u32[]{:S(2)}, u32[]{:S(2)}) collective-permute-start(bf16[1024,128]{1,0:T(8,128)(2,1)} %bitcast.8), channel_id=1, source_target_pairs={{0,4},{2,6},{4,8},{6,10},{8,12},{10,14},{12,16},{14,18},{16,20},{1... | collective-permute-start | bytes 786440 | tf_op jit(solution)/shard_map/ppermute | solution.py:10
  85.8 20.6 %collective-permute-start.11 = (bf16[1024,128]{1,0:T(8,128)(2,1)}, bf16[1024,128]{1,0:T(8,128)(2,1)S(1)}, u32[]{:S(2)}, u32[]{:S(2)}) collective-permute-start(bf16[1024,128]{1,0:T(8,128)(2,1)} %bitcast.8), channel_id=1, source_target_pairs={{0,2},{2,4},{4,6},{6,8},{8,10},{10,12},{12,14},{14,16},{16,18},{18... | collective-permute-start | bytes 786440 | tf_op jit(solution)/shard_map/ppermute | solution.py:10
  101.8 11.5 %collective-permute-start.2 = (bf16[1024,128]{1,0:T(8,128)(2,1)S(1)}, bf16[1024,128]{1,0:T(8,128)(2,1)S(1)}, u32[]{:S(2)}, u32[]{:S(2)}) collective-permute-start(bf16[1024,128]{1,0:T(8,128)(2,1)S(1)} %get-tuple-element.49), channel_id=1, source_target_pairs={{0,4},{2,6},{4,8},{6,10},{8,12},{10,14},{12,16},{14,18},{16,20},{1... | collective-permute-start | bytes 786440 | tf_op jit(solution)/shard_map/ppermute | solution.py:10
  101.9 13.4 %collective-permute-start.3 = (bf16[1024,128]{1,0:T(8,128)(2,1)S(1)}, bf16[1024,128]{1,0:T(8,128)(2,1)S(1)}, u32[]{:S(2)}, u32[]{:S(2)}) collective-permute-start(bf16[1024,128]{1,0:T(8,128)(2,1)S(1)} %get-tuple-element.50), channel_id=1, source_target_pairs={{0,28},{2,30},{4,0},{6,2},{8,4},{10,6},{12,8},{14,10},{16,12},{18,... | collective-permute-start | bytes 786440 | tf_op jit(solution)/shard_map/ppermute | solution.py:10
  106.0 12.0 %collective-permute-start.12 = (bf16[1024,128]{1,0:T(8,128)(2,1)}, bf16[1024,128]{1,0:T(8,128)(2,1)}, u32[]{:S(2)}, u32[]{:S(2)}) collective-permute-start(bf16[1024,128]{1,0:T(8,128)(2,1)} %bitcast.8), channel_id=1, source_target_pairs={{0,24},{2,26},{4,28},{6,30},{8,0},{10,2},{12,4},{14,6},{16,8},{18,... | collective-permute-start | bytes 786440 | tf_op jit(solution)/shard_map/ppermute | solution.py:10
  106.4 17.3 %collective-permute-start.13 = (bf16[1024,128]{1,0:T(8,128)(2,1)}, bf16[1024,128]{1,0:T(8,128)(2,1)}, u32[]{:S(2)}, u32[]{:S(2)}) collective-permute-start(bf16[1024,128]{1,0:T(8,128)(2,1)} %bitcast.8), channel_id=1, source_target_pairs={{0,28},{2,30},{4,0},{6,2},{8,4},{10,6},{12,8},{14,10},{16,12},{18,... | collective-permute-start | bytes 786440 | tf_op jit(solution)/shard_map/ppermute | solution.py:10
  106.4 17.7 %collective-permute-start.14 = (bf16[1024,128]{1,0:T(8,128)(2,1)}, bf16[1024,128]{1,0:T(8,128)(2,1)}, u32[]{:S(2)}, u32[]{:S(2)}) collective-permute-start(bf16[1024,128]{1,0:T(8,128)(2,1)} %bitcast.8), channel_id=1, source_target_pairs={{0,30},{2,0},{4,2},{6,4},{8,6},{10,8},{12,10},{14,12},{16,14},{18,... | collective-permute-start | bytes 786440 | tf_op jit(solution)/shard_map/ppermute | solution.py:10
  113.3 32.8 %collective-permute-start.8 = (bf16[1024,128]{1,0:T(8,128)(2,1)}, bf16[1024,128]{1,0:T(8,128)(2,1)S(1)}, u32[]{:S(2)}, u32[]{:S(2)}) collective-permute-start(bf16[1024,128]{1,0:T(8,128)(2,1)} %bitcast.8), channel_id=1, source_target_pairs={{0,16},{2,18},{4,20},{6,22},{8,24},{10,26},{12,28},{14,30},{16,0},... | collective-permute-start | bytes 786440 | tf_op jit(solution)/shard_map/ppermute | solution.py:10
  115.3 30.8 %collective-permute-start.9 = (bf16[1024,128]{1,0:T(8,128)(2,1)}, bf16[1024,128]{1,0:T(8,128)(2,1)S(1)}, u32[]{:S(2)}, u32[]{:S(2)}) collective-permute-start(bf16[1024,128]{1,0:T(8,128)(2,1)} %bitcast.8), channel_id=1, source_target_pairs={{0,8},{2,10},{4,12},{6,14},{8,16},{10,18},{12,20},{14,22},{16,24},... | collective-permute-start | bytes 786440 | tf_op jit(solution)/shard_map/ppermute | solution.py:10
  118.0 29.1 %collective-permute-start.4 = (bf16[1024,128]{1,0:T(8,128)(2,1)S(1)}, bf16[1024,128]{1,0:T(8,128)(2,1)S(1)}, u32[]{:S(2)}, u32[]{:S(2)}) collective-permute-start(bf16[1024,128]{1,0:T(8,128)(2,1)S(1)} %get-tuple-element.51), channel_id=1, source_target_pairs={{0,8},{2,10},{4,12},{6,14},{8,16},{10,18},{12,20},{14,22},{16,24},... | collective-permute-start | bytes 786440 | tf_op jit(solution)/shard_map/ppermute | solution.py:10
  123.7 23.4 %collective-permute-start.5 = (bf16[1024,128]{1,0:T(8,128)(2,1)S(1)}, bf16[1024,128]{1,0:T(8,128)(2,1)}, u32[]{:S(2)}, u32[]{:S(2)}) collective-permute-start(bf16[1024,128]{1,0:T(8,128)(2,1)S(1)} %get-tuple-element.52), channel_id=1, source_target_pairs={{0,24},{2,26},{4,28},{6,30},{8,0},{10,2},{12,4},{14,6},{16,8},{18,... | collective-permute-start | bytes 786440 | tf_op jit(solution)/shard_map/ppermute | solution.py:10
  146.2 1.9 copy-start
  148.3 27.0 %collective-permute-start.6 = (bf16[1024,128]{1,0:T(8,128)(2,1)S(1)}, bf16[1024,128]{1,0:T(8,128)(2,1)S(1)}, u32[]{:S(2)}, u32[]{:S(2)}) collective-permute-start(bf16[1024,128]{1,0:T(8,128)(2,1)S(1)} %get-tuple-element.53), channel_id=1, source_target_pairs={{0,16},{2,18},{4,20},{6,22},{8,24},{10,26},{12,28},{14,30},{16,0},... | collective-permute-start | bytes 786440 | tf_op jit(solution)/shard_map/ppermute | solution.py:10
  159.9 20.7 %collective-permute-start.7 = (bf16[1024,128]{1,0:T(8,128)(2,1)S(1)}, bf16[1024,128]{1,0:T(8,128)(2,1)S(1)}, u32[]{:S(2)}, u32[]{:S(2)}) collective-permute-start(bf16[1024,128]{1,0:T(8,128)(2,1)S(1)} %get-tuple-element.54), channel_id=1, source_target_pairs={{0,16},{2,18},{4,20},{6,22},{8,24},{10,26},{12,28},{14,30},{16,0},... | collective-permute-start | bytes 786440 | tf_op jit(solution)/shard_map/ppermute | solution.py:10
  180.7 12.5 %copy-start.5 = (bf16[1024,128]{1,0:T(8,128)(2,1)}, bf16[1024,128]{1,0:T(8,128)(2,1)S(1)}, u32[]{:S(2)}) copy-start(bf16[1024,128]{1,0:T(8,128)(2,1)S(1)} %subtract_convert_fusion) | copy-start | bytes 786436
Sparse Core Ops, SparseCore 0:
  9.6 35.1 all-gather.3
  46.3 33.1 all-gather.5
  147.2 20.0 all-gather.7
where the time goes:
time: 201 us; the launch traced here: 200 us
  waiting for transfers between devices  142 us (71%)
  starting transfers between devices  29.2 us (15%)
  between operations  13.9 us (7%)
  blocking collectives  7.28 us (4%)
  matrix products  5 us (2%)
  other arithmetic  2.21 us (1%)
    ppermute x15, waiting for transfers between devices, shifted(): return lax.ppermute(value, axis, pairs)  69.4 us
    all_gather x1, waiting for transfers between devices, body(): lax.all_gather(lower_coupling, 'cols', axis=1, tiled=True)  36 us
    all_gather x1, waiting for transfers between devices, body(): lax.all_gather(upper_coupling, 'cols', axis=1, tiled=True)  34.7 us
    ppermute x15, starting transfers between devices, shifted(): return lax.ppermute(value, axis, pairs)  29.1 us
    all_to_all x1, blocking collectives, body(): lax.all_to_all(factor, 'cols', split_axis=0, concat_axis=1, tiled=True)  7.28 us
  transfers between devices with their start and end apart: 18, of which 11 were waited for; matrix products, arithmetic and copies ran while one was open for 1% of the time, Pallas kernels for 0%

commit v1 on v0

v1 whole, which is shorter than its diff:
```python
import functools

import jax
import jax.numpy as jnp
from jax import lax
from jax.experimental import pallas as pl
from jax.experimental.pallas import tpu as pltpu
from jax.sharding import PartitionSpec as P

MESH = pl.DeviceIdType.MESH
F32 = jnp.float32
BF16 = jnp.bfloat16


def kernel(n, nx, lower_hbm, upper_hbm, sol_hbm, cot_hbm, src_out, low_out, up_out,
           low_v, up_v, sol_v, cot_v, cot_t, cot_half, acc, factor_t, factor, push_out,
           push_in, root_out, root_in, near, src_t, src_v, grad_v,
           load_sem, store_sem, cot_ss, cot_rs, push_ss, push_rs, root_ss, root_rs,
           sol_ss, sol_rs, near_ss, near_rs, src_ss, src_rs):
    block, width = cot_v.shape
    half = block // nx
    levels = n.bit_length() - 1
    last = levels - 1
    row = lax.axis_index("rows")
    col = lax.axis_index("cols")
    offset = lax.rem(row + n - 1, n)
    level = jnp.int32(0)
    for l in range(levels):
        level = level + jnp.where(lax.rem(offset, 2 << l) == 0, 1, 0)
    is_root = level == levels
    is_last = level == last
    stride = jnp.int32(1)
    for l in range(levels):
        stride = jnp.where(level > l, 2 << l, stride)
    stride = jnp.where(is_root, 0, stride)

    def other(k):
        return lax.rem(col + k, nx)

    def up_row(s):
        return lax.rem(row + s, n)

    def down_row(s):
        return lax.rem(row + n - s, n)

    loads = [
        pltpu.make_async_copy(cot_hbm.at[0], cot_v, load_sem.at[0]),
        pltpu.make_async_copy(lower_hbm.at[0], low_v, load_sem.at[1]),
        pltpu.make_async_copy(upper_hbm.at[0], up_v, load_sem.at[2]),
        pltpu.make_async_copy(sol_hbm.at[0], sol_v, load_sem.at[3]),
    ]
    for load in loads:
        load.start()

    barrier = pltpu.get_barrier_semaphore()
    for k in range(1, nx):
        pl.semaphore_signal(barrier, inc=1, device_id=(row, other(k)), device_id_type=MESH)
    for l in range(levels):
        @pl.when(level >= l)
        def _():
            for k in range(nx):
                pl.semaphore_signal(barrier, inc=1, device_id=(up_row(1 << l), k), device_id_type=MESH)
                if l != last:
                    pl.semaphore_signal(barrier, inc=1, device_id=(down_row(1 << l), k), device_id_type=MESH)

    loads[0].wait()
    cot_t[...] = cot_v[...].T
    low_half = pl.ds(pl.multiple_of(col * half, half), half)
    own_cols = pl.ds(pl.multiple_of(col * width, width), width)
    cot_half[own_cols, :] = cot_t[:, low_half]

    reached = jnp.minimum(level + 1, last)
    pl.semaphore_wait(barrier, (nx - 1) + nx * (2 * reached + jnp.where(level >= last, 1, 0)))

    def cot_copy(k):
        to = other(k)
        return pltpu.make_async_remote_copy(
            src_ref=cot_t.at[:, pl.ds(pl.multiple_of(to * half, half), half)],
            dst_ref=cot_half.at[own_cols, :],
            send_sem=cot_ss.at[k], recv_sem=cot_rs.at[k],
            device_id=(row, to), device_id_type=MESH)

    for k in range(1, nx):
        cot_copy(k).start()

    loads[3].wait()

    def sol_copy(l, d):
        target = up_row(1 << l) if d == 0 else down_row(1 << l)
        return pltpu.make_async_remote_copy(
            src_ref=sol_v, dst_ref=near.at[d, col],
            send_sem=sol_ss.at[l, d], recv_sem=sol_rs.at[d],
            device_id=(target, col), device_id_type=MESH)

    def each_sol(act):
        for l in range(levels):
            @pl.when(level > l)
            def _():
                for d in range(2 if l != last else 1):
                    act(sol_copy(l, d))

    each_sol(lambda c: c.start())

    def near_copy(d, k):
        return pltpu.make_async_remote_copy(
            src_ref=near.at[d, col], dst_ref=near.at[d, col],
            send_sem=near_ss.at[d, k], recv_sem=near_rs.at[d, k],
            device_id=(row, other(k)), device_id_type=MESH)

    def each_near(act):
        act(0)

        @pl.when(level < last)
        def _():
            act(1)

    def forward_near():
        def act(d):
            sol_copy(0, d).wait_recv()
            for k in range(1, nx):
                near_copy(d, k).start()
        each_near(act)

    for k in range(1, nx):
        cot_copy(k).wait_recv()
    acc[...] = cot_half[...].astype(F32)

    def push_copy(l, d, k, target):
        to = other(k)
        return pltpu.make_async_remote_copy(
            src_ref=push_out.at[d, to], dst_ref=push_in.at[l, d, col],
            send_sem=push_ss.at[d, k], recv_sem=push_rs.at[l, d, col],
            device_id=(target, to), device_id_type=MESH)

    for l in range(last):
        @pl.when(level > l)
        def _():
            for c in range(nx):
                for d in range(2):
                    pltpu.make_async_remote_copy(
                        src_ref=push_out.at[d, c], dst_ref=push_in.at[l, d, c],
                        send_sem=push_ss.at[d, c], recv_sem=push_rs.at[l, d, c],
                        device_id=(row, other(1)), device_id_type=MESH).wait_recv()
            total = push_in[l, 0, 0].astype(F32)
            for d in range(2):
                for c in range(nx):
                    if d + c:
                        total = total + push_in[l, d, c].astype(F32)
            acc[...] = acc[...] - total
            if l == 0:
                @pl.when(jnp.logical_not(is_root))
                def _():
                    forward_near()

    factor_t[...] = acc[...].astype(BF16)
    loads[1].wait()
    loads[2].wait()

    my_level = jnp.minimum(level, last - 1) if last else jnp.int32(0)

    @pl.when(level < last)
    def _():
        for k in list(range(1, nx)) + [0]:
            to = other(k)
            part = pl.ds(pl.multiple_of(to * half, half), half)
            for d, mat in ((1, low_v), (0, up_v)):
                push_out[d, to] = jnp.dot(
                    factor_t[...], mat[:, part], preferred_element_type=F32).astype(BF16)
                target = up_row(stride) if d == 0 else down_row(stride)
                push_copy(my_level, d, k, target).start()

    def root_copy(k):
        to = other(k)
        return pltpu.make_async_remote_copy(
            src_ref=root_out.at[to], dst_ref=root_in.at[col],
            send_sem=root_ss.at[k], recv_sem=root_rs.at[col],
            device_id=(up_row(1 << last), to), device_id_type=MESH)

    @pl.when(is_last)
    def _():
        for k in list(range(1, nx)) + [0]:
            to = other(k)
            rows = pl.ds(pl.multiple_of(to * width, width), width)
            both = jnp.dot(factor_t[rows, :], low_v[...], preferred_element_type=F32)
            both = both + jnp.dot(factor_t[rows, :], up_v[...], preferred_element_type=F32)
            root_out[to] = both.astype(BF16)
            root_copy(k).start()

    def src_copy(k):
        to = other(k)
        return pltpu.make_async_remote_copy(
            src_ref=factor_t.at[pl.ds(pl.multiple_of(to * width, width), width), :],
            dst_ref=src_t.at[:, low_half],
            send_sem=src_ss.at[k], recv_sem=src_rs.at[k],
            device_id=(row, to), device_id_type=MESH)

    for k in range(1, nx):
        src_copy(k).start()
    src_t[:, low_half] = factor_t[own_cols, :]

    @pl.when(level == 0)
    def _():
        forward_near()

    low_store = pltpu.make_async_copy(grad_v.at[0], low_out.at[0], store_sem.at[0])
    up_store = pltpu.make_async_copy(grad_v.at[1], up_out.at[0], store_sem.at[1])
    src_store = pltpu.make_async_copy(src_v, src_out.at[0], store_sem.at[2])

    @pl.when(is_root)
    def _():
        grad_v[...] = jnp.zeros_like(grad_v)

    @pl.when(jnp.logical_not(is_root))
    def _():
        factor[...] = -(factor_t[...].T)

        def act(d):
            for k in range(1, nx):
                near_copy(d, k).wait_recv()
        each_near(act)
        for d in range(2):
            which = d if d == 0 else jnp.where(is_last, 0, 1)
            full = jnp.concatenate([near[which, c] for c in range(nx)], axis=1)
            grad_v[d] = lax.dot_general(
                factor[...], full, (((1,), (1,)), ((), ())),
                preferred_element_type=F32).astype(BF16)

    low_store.start()
    up_store.start()

    for k in range(1, nx):
        src_copy(k).wait_recv()

    @pl.when(is_root)
    def _():
        total = src_t[...].astype(F32)
        for c in range(nx):
            pltpu.make_async_remote_copy(
                src_ref=root_out.at[c], dst_ref=root_in.at[c],
                send_sem=root_ss.at[c], recv_sem=root_rs.at[c],
                device_id=(row, other(1)), device_id_type=MESH).wait_recv()
        for c in range(nx):
            total = total - root_in[c].astype(F32)
        src_t[...] = total.astype(BF16)

    src_v[...] = src_t[...].T
    src_store.start()

    for k in range(1, nx):
        cot_copy(k).wait_send()
        src_copy(k).wait_send()
    each_sol(lambda c: c.wait_send())

    @pl.when(jnp.logical_not(is_root))
    def _():
        def act(d):
            for k in range(1, nx):
                near_copy(d, k).wait_send()
        each_near(act)

    @pl.when(level < last)
    def _():
        for k in range(nx):
            for d in range(2):
                push_copy(my_level, d, k, up_row(stride)).wait_send()

    @pl.when(is_last)
    def _():
        for k in range(nx):
            root_copy(k).wait_send()

    low_store.wait()
    up_store.wait()
    src_store.wait()


def body(n, nx, lower_coupling, upper_coupling, solution, cotangent):
    _, half, block = lower_coupling.shape
    width = cotangent.shape[2]
    full = width * nx
    levels = n.bit_length() - 1
    dma = pltpu.SemaphoreType.DMA
    return pl.pallas_call(
        functools.partial(kernel, n, nx),
        out_shape=(
            jax.ShapeDtypeStruct(cotangent.shape, BF16),
            jax.ShapeDtypeStruct(lower_coupling.shape, BF16),
            jax.ShapeDtypeStruct(upper_coupling.shape, BF16),
        ),
        in_specs=[pl.BlockSpec(memory_space=pl.ANY)] * 4,
        out_specs=[pl.BlockSpec(memory_space=pl.ANY)] * 3,
        scratch_shapes=[
            pltpu.VMEM((half, block), BF16),
            pltpu.VMEM((half, block), BF16),
            pltpu.VMEM((block, width), BF16),
            pltpu.VMEM((block, width), BF16),
            pltpu.VMEM((width, block), BF16),
            pltpu.VMEM((full, half), BF16),
            pltpu.VMEM((full, half), F32),
            pltpu.VMEM((full, half), BF16),
            pltpu.VMEM((half, full), BF16),
            pltpu.VMEM((2, nx, full, half), BF16),
            pltpu.VMEM((max(levels - 1, 1), 2, nx, full, half), BF16),
            pltpu.VMEM((nx, width, block), BF16),
            pltpu.VMEM((nx, width, block), BF16),
            pltpu.VMEM((2, nx, block, width), BF16),
            pltpu.VMEM((width, block), BF16),
            pltpu.VMEM((block, width), BF16),
            pltpu.VMEM((2, half, block), BF16),
            dma((4,)), dma((3,)),
            dma((nx,)), dma((nx,)),
            dma((2, nx)), dma((max(levels - 1, 1), 2, nx)),
            dma((nx,)), dma((nx,)),
            dma((levels, 2)), dma((2,)),
            dma((2, nx)), dma((2, nx)),
            dma((nx,)), dma((nx,)),
        ],
        compiler_params=pltpu.CompilerParams(
            collective_id=0, has_side_effects=True, vmem_limit_bytes=48 * 1024 * 1024),
    )(lower_coupling, upper_coupling, solution, cotangent)


def solution(mesh):
    in_specs = (
        P("rows", "cols", None),
        P("rows", "cols", None),
        P("rows", None, "cols"),
        P("rows", None, "cols"),
    )
    out_specs = (P("rows", None, "cols"), P("rows", "cols", None), P("rows", "cols", None))
    local = functools.partial(body, mesh.shape["rows"], mesh.shape["cols"])
    return jax.shard_map(local, mesh=mesh, in_specs=in_specs, out_specs=out_specs, check_vma=False)
```

time: 201 us -> 67.1 us (0.33)
  waiting for transfers between devices: 142 us -> 0 us
  Pallas kernels: 0 us -> 59.2 us
  starting transfers between devices: 29.2 us -> 0 us
  between operations: 13.9 us -> 0.65 us
  blocking collectives: 7.28 us -> 0 us
  local copies, waits for them, and re-layouts: 0.45 us -> 6.99 us
  matrix products: 5 us -> 0 us
  other arithmetic: 2.21 us -> 0 us
    all_gather x3 -> x0, waiting for transfers between devices: 70.8 us -> none  [the longest x1 36 us: body(): lax.all_gather(lower_coupling, 'cols', axis=1, tiled=True)]
    ppermute x15 -> x0, waiting for transfers between devices: 69.4 us -> none  [shifted(): return lax.ppermute(value, axis, pairs)]
    pallas_call x0 -> x1, Pallas kernels: none -> 59.2 us  [body(): pl.pallas_call(functools.partial(kernel, n, nx), out_shape=(jax.ShapeDtyp...]
    ppermute x15 -> x0, starting transfers between devices: 29.1 us -> none  [shifted(): return lax.ppermute(value, axis, pairs)]
    all_to_all x1 -> x0, blocking collectives: 7.28 us -> none  [body(): lax.all_to_all(factor, 'cols', split_axis=0, concat_axis=1, tiled=True)]
    unnamed x6 -> x11, local copies, waits for them, and re-layouts: 0.02 us -> 6.99 us
    dot_general x2 -> x0, matrix products: 5 us -> none  [the longest x1 2.5 us: body(): lax.dot_general(half_rows, neighbours[1], contract, preferred_element_typ...]
  transfers between devices with their start and end apart: 18 -> 0, of which waited for: 11 -> 0; matrix products, arithmetic and copies ran while one was open for 1% -> 0% of each run, Pallas kernels for 0% -> 0%
where the time goes in v1:
time: 67.1 us; the launch traced here: 66.8 us
  Pallas kernels  59.2 us (88%)
  local copies, waits for them, and re-layouts  6.99 us (10%)
    pallas_call x1, Pallas kernels, body(): pl.pallas_call(functools.partial(kernel, n, nx), out_shape=(jax.ShapeDtyp...  59.2 us
    unnamed x11, local copies, waits for them, and re-layouts  6.99 us

profile of v1, /device:TPU:1, one launch (start us, length us, event | category | flops | bytes accessed | tf_op | source)
XLA Modules:
  0.0 66.8 jit_solution(17638729793352525743)
XLA Ops:
  0.6 0.0 copy-start
  0.6 1.2 %copy-done = bf16[1,512,1024]{2,1,0:T(8,128)(2,1)S(1)} copy-done((bf16[1,512,1024]{2,1,0:T(8,128)(2,1)S(1)}, bf16[1,512,1024]{2,1,0:T(8,128)(2,1)}, u32[]{:S(2)}) %copy-start) | copy-done | bytes 1048600
  1.9 0.0 copy-start.1
  1.9 1.2 %copy-done.1 = bf16[1,512,1024]{2,1,0:T(8,128)(2,1)S(1)} copy-done((bf16[1,512,1024]{2,1,0:T(8,128)(2,1)S(1)}, bf16[1,512,1024]{2,1,0:T(8,128)(2,1)}, u32[]{:S(2)}) %copy-start.1) | copy-done | bytes 1048600
  3.1 0.0 copy-start.2
  3.1 0.9 %copy-done.2 = bf16[1,1024,128]{2,1,0:T(8,128)(2,1)S(1)} copy-done((bf16[1,1024,128]{2,1,0:T(8,128)(2,1)S(1)}, bf16[1,1024,128]{2,1,0:T(8,128)(2,1)}, u32[]{:S(2)}) %copy-start.2) | copy-done | bytes 262168
  4.0 0.0 copy-start.3
  4.0 0.9 %copy-done.3 = bf16[1,1024,128]{2,1,0:T(8,128)(2,1)S(1)} copy-done((bf16[1,1024,128]{2,1,0:T(8,128)(2,1)S(1)}, bf16[1,1024,128]{2,1,0:T(8,128)(2,1)}, u32[]{:S(2)}) %copy-start.3) | copy-done | bytes 262168
  5.0 59.2 %shard_map.67 = (bf16[1,1024,128]{2,1,0:T(8,128)(2,1)S(1)}, bf16[1,512,1024]{2,1,0:T(8,128)(2,1)S(1)}, bf16[1,512,1024]{2,1,0:T(8,128)(2,1)S(1)}) custom-call(bf16[1,512,1024]{2,1,0:T(8,128)(2,1)S(1)} %copy-done, bf16[1,512,1024]{2,1,0:T(8,128)(2,1)S(1)} %copy-done.1, bf16[1,1024,128]{2,1,0:T(8,128)(2,1)S(1)} %copy-done.2, bf16[1,1024,128]{2,1,0:T(8,128)(2,1)S(1)} %copy-done.3), custom_call_target="tpu_custom_call" | custom-call | tf_op jit(solution)/shard_map/pallas_call | solution.py:283
  64.2 0.7 %copy.10 = bf16[1,1024,128]{2,1,0:T(8,128)(2,1)} copy(bf16[1,1024,128]{2,1,0:T(8,128)(2,1)S(1)} %get-tuple-element.6) | data formatting | bytes 524288
  64.9 1.0 %copy.11 = bf16[1,512,1024]{2,1,0:T(8,128)(2,1)} copy(bf16[1,512,1024]{2,1,0:T(8,128)(2,1)S(1)} %get-tuple-element.7) | data formatting | bytes 2097152
  65.9 1.0 %copy.12 = bf16[1,512,1024]{2,1,0:T(8,128)(2,1)} copy(bf16[1,512,1024]{2,1,0:T(8,128)(2,1)S(1)} %get-tuple-element.8) | data formatting | bytes 2097152
Async XLA Ops:
  0.6 1.2 %copy-start = (bf16[1,512,1024]{2,1,0:T(8,128)(2,1)S(1)}, bf16[1,512,1024]{2,1,0:T(8,128)(2,1)}, u32[]{:S(2)}) copy-start(bf16[1,512,1024]{2,1,0:T(8,128)(2,1)} %lower_hbm.1) | copy-start | bytes 3145732
  1.9 1.2 %copy-start.1 = (bf16[1,512,1024]{2,1,0:T(8,128)(2,1)S(1)}, bf16[1,512,1024]{2,1,0:T(8,128)(2,1)}, u32[]{:S(2)}) copy-start(bf16[1,512,1024]{2,1,0:T(8,128)(2,1)} %upper_hbm.1) | copy-start | bytes 3145732
  3.1 0.9 %copy-start.2 = (bf16[1,1024,128]{2,1,0:T(8,128)(2,1)S(1)}, bf16[1,1024,128]{2,1,0:T(8,128)(2,1)}, u32[]{:S(2)}) copy-start(bf16[1,1024,128]{2,1,0:T(8,128)(2,1)} %sol_hbm.1) | copy-start | bytes 786436
  4.0 0.9 %copy-start.3 = (bf16[1,1024,128]{2,1,0:T(8,128)(2,1)S(1)}, bf16[1,1024,128]{2,1,0:T(8,128)(2,1)}, u32[]{:S(2)}) copy-start(bf16[1,1024,128]{2,1,0:T(8,128)(2,1)} %cot_hbm.1) | copy-start | bytes 786436

commit v2 on v1

v2 whole, which is shorter than its diff:
```python
import functools

import jax
import jax.numpy as jnp
from jax import lax
from jax.experimental import pallas as pl
from jax.experimental.pallas import tpu as pltpu
from jax.sharding import PartitionSpec as P

MESH = pl.DeviceIdType.MESH
F32 = jnp.float32
BF16 = jnp.bfloat16


def kernel(n, nx, wide, lower_hbm, upper_hbm, sol_hbm, cot_hbm, src_out, low_out, up_out,
           mats, sol_v, cot_v, cot_t, cot_half, acc, factor_t, factor, half_out, half_in,
           acc_col, col_out, col_in, wide_out, wide_in, near, src_t, src_v, grad_v,
           load_sem, store_sem, cot_ss, cot_rs, half_ss, half_rs, col_ss, col_rs,
           wide_ss, wide_rs, gat_ss, gat_rs, sol_ss, sol_rs, near_ss, near_rs, src_ss, src_rs):
    block, width = cot_v.shape
    half = block // nx
    levels = n.bit_length() - 1
    last = levels - 1
    row = lax.axis_index("rows")
    col = lax.axis_index("cols")
    offset = lax.rem(row + n - 1, n)
    level = jnp.int32(0)
    for l in range(levels):
        level = level + jnp.where(lax.rem(offset, 2 << l) == 0, 1, 0)
    is_root = level == levels
    is_last = level == last
    is_half = level < wide
    is_col = (level >= wide) & (level < levels)
    stride = jnp.int32(1)
    for l in range(levels):
        stride = jnp.where(level > l, 2 << l, stride)
    stride = jnp.where(is_root, 0, stride)

    def other(k):
        return lax.rem(col + k, nx)

    def up_row(s):
        return lax.rem(row + s, n)

    def down_row(s):
        return lax.rem(row + n - s, n)

    loads = [
        pltpu.make_async_copy(cot_hbm.at[0], cot_v, load_sem.at[0]),
        pltpu.make_async_copy(lower_hbm.at[0], mats.at[1, col], load_sem.at[1]),
        pltpu.make_async_copy(upper_hbm.at[0], mats.at[0, col], load_sem.at[2]),
        pltpu.make_async_copy(sol_hbm.at[0], sol_v, load_sem.at[3]),
    ]
    for load in loads:
        load.start()

    barrier = pltpu.get_barrier_semaphore()
    for k in range(1, nx):
        pl.semaphore_signal(barrier, inc=1, device_id=(row, other(k)), device_id_type=MESH)
    for l in range(levels):
        @pl.when(level >= l)
        def _():
            for k in range(nx):
                pl.semaphore_signal(barrier, inc=1, device_id=(up_row(1 << l), k), device_id_type=MESH)
                if l != last:
                    pl.semaphore_signal(barrier, inc=1, device_id=(down_row(1 << l), k), device_id_type=MESH)

    loads[0].wait()
    cot_t[...] = cot_v[...].T
    low_half = pl.ds(pl.multiple_of(col * half, half), half)
    own_cols = pl.ds(pl.multiple_of(col * width, width), width)

    @pl.when(is_half)
    def _():
        cot_half[own_cols, :] = cot_t[:, low_half]

    reached = jnp.minimum(level + 1, last)
    pl.semaphore_wait(barrier, (nx - 1) + nx * (2 * reached + jnp.where(level >= last, 1, 0)))

    def cot_copy(k):
        to = other(k)
        return pltpu.make_async_remote_copy(
            src_ref=cot_t.at[:, pl.ds(pl.multiple_of(to * half, half), half)],
            dst_ref=cot_half.at[own_cols, :],
            send_sem=cot_ss.at[k], recv_sem=cot_rs.at[k],
            device_id=(row, to), device_id_type=MESH)

    def gather_copy(d, k):
        return pltpu.make_async_remote_copy(
            src_ref=(upper_hbm, lower_hbm)[d].at[0], dst_ref=mats.at[d, col],
            send_sem=gat_ss.at[d, k], recv_sem=gat_rs.at[d, k],
            device_id=(row, other(k)), device_id_type=MESH)

    @pl.when(is_half)
    def _():
        for k in range(1, nx):
            cot_copy(k).start()

    @pl.when(is_col)
    def _():
        for d in range(2):
            for k in range(1, nx):
                gather_copy(d, k).start()

    def sol_copy(l, d):
        target = up_row(1 << l) if d == 0 else down_row(1 << l)
        return pltpu.make_async_remote_copy(
            src_ref=sol_v, dst_ref=near.at[d, col],
            send_sem=sol_ss.at[l, d], recv_sem=sol_rs.at[d],
            device_id=(target, col), device_id_type=MESH)

    def each_sol(act):
        for l in range(levels):
            @pl.when(level > l)
            def _():
                for d in range(2 if l != last else 1):
                    act(sol_copy(l, d))


    def near_copy(d, k):
        return pltpu.make_async_remote_copy(
            src_ref=near.at[d, col], dst_ref=near.at[d, col],
            send_sem=near_ss.at[d, k], recv_sem=near_rs.at[d, k],
            device_id=(row, other(k)), device_id_type=MESH)

    def each_near(act):
        act(0)

        @pl.when(level < last)
        def _():
            act(1)

    def forward_near():
        def act(d):
            sol_copy(0, d).wait_recv()
            for k in range(1, nx):
                near_copy(d, k).start()
        each_near(act)

    def send_sol():
        each_sol(lambda c: c.start())

    def half_copy(k, l, d, target):
        to = other(k)
        return pltpu.make_async_remote_copy(
            src_ref=half_out.at[to], dst_ref=half_in.at[l, d, col],
            send_sem=half_ss.at[k], recv_sem=half_rs.at[l, d, col],
            device_id=(target, to), device_id_type=MESH)

    def col_copy(k, l, d, target):
        to = other(k)
        return pltpu.make_async_remote_copy(
            src_ref=col_out.at[d, to], dst_ref=col_in.at[l, d, col],
            send_sem=col_ss.at[d, k], recv_sem=col_rs.at[l, d, col],
            device_id=(target, to), device_id_type=MESH)

    def wide_copy(j, l, d, target):
        return pltpu.make_async_remote_copy(
            src_ref=wide_out.at[d, j], dst_ref=wide_in.at[l, d, j],
            send_sem=wide_ss.at[d, j], recv_sem=wide_rs.at[l, d, j],
            device_id=(target, col), device_id_type=MESH)

    def arrived(dst, sem):
        pltpu.make_async_remote_copy(
            src_ref=dst, dst_ref=dst, send_sem=sem, recv_sem=sem,
            device_id=(row, other(1)), device_id_type=MESH).wait_recv()

    def src_copy(k):
        to = other(k)
        return pltpu.make_async_remote_copy(
            src_ref=factor_t.at[pl.ds(pl.multiple_of(to * width, width), width), :],
            dst_ref=src_t.at[:, low_half],
            send_sem=src_ss.at[k], recv_sem=src_rs.at[k],
            device_id=(row, to), device_id_type=MESH)

    span = jnp.maximum(stride, 1)
    first = jnp.where(lax.rem(offset + span, 4 * span) == 2 * span, 0, 1)
    second = 1 - first

    def target_of(d):
        return jnp.where(d == 0, up_row(stride), down_row(stride))

    order = list(range(1, nx)) + [0]
    half_level = jnp.minimum(level, wide - 1)

    def fill_col(d):
        push = jnp.dot(factor_t[...], mats[d, col], preferred_element_type=F32).astype(BF16)
        for c in range(nx):
            col_out[d, c] = push[c * width:(c + 1) * width]

    @pl.when(is_half)
    def _():
        for k in range(1, nx):
            cot_copy(k).wait_recv()

        @pl.when(level == 0)
        def _():
            factor_t[...] = cot_half[...]

        for l in range(wide - 1):
            @pl.when(level > l)
            def _():
                if l == 0:
                    acc[...] = cot_half[...].astype(F32)
                total = None
                for c in range(nx):
                    for d in range(2):
                        arrived(half_in.at[l, d, c], half_rs.at[l, d, c])
                        term = half_in[l, d, c].astype(F32)
                        total = term if total is None else total + term
                acc[...] = acc[...] - total
                factor_t[...] = acc[...].astype(BF16)

        loads[1].wait()
        loads[2].wait()

        @pl.when(level < wide - 1)
        def _():
            for k in order:
                to = other(k)
                part = pl.ds(pl.multiple_of(to * half, half), half)
                half_out[to] = jnp.dot(
                    factor_t[...], mats[first, col, :, part], preferred_element_type=F32).astype(BF16)
                half_copy(k, jnp.minimum(half_level, max(wide - 2, 0)), first, target_of(first)).start()

        @pl.when(level == wide - 1)
        def _():
            fill_col(first)
            for k in order:
                col_copy(k, half_level, first, target_of(first)).start()

        fill_col(second)
        for k in order:
            col_copy(k, half_level, second, target_of(second)).start()
        for k in range(1, nx):
            src_copy(k).start()
        src_t[:, low_half] = factor_t[own_cols, :]
        loads[3].wait()
        send_sol()
        forward_near()

    @pl.when(level >= wide)
    def _():
        acc_col[...] = cot_t[...].astype(F32)
        for l in range(wide):
            total = None
            for c in range(nx):
                for d in range(2):
                    arrived(col_in.at[l, d, c], col_rs.at[l, d, c])
                    term = col_in[l, d, c].astype(F32)
                    total = term if total is None else total + term
            acc_col[...] = acc_col[...] - total
            if l == 0:
                loads[3].wait()
                send_sol()
        loads[1].wait()
        loads[2].wait()

        @pl.when((level > wide) & (level < levels))
        def _():
            forward_near()

        def add_wide(l, ds):
            for j in range(nx):
                total = None
                for d in ds:
                    arrived(wide_in.at[l, d, j], wide_rs.at[l, d, j])
                    term = wide_in[l, d, j].astype(F32)
                    total = term if total is None else total + term
                part = slice(j * half, (j + 1) * half)
                acc_col[:, part] = acc_col[:, part] - total

        for l in range(wide, last):
            @pl.when(level > l)
            def _():
                add_wide(l - wide, (0, 1))

        @pl.when(is_root)
        def _():
            add_wide(last - wide, (0,))
            src_t[...] = acc_col[...].astype(BF16)

    wide_level = jnp.maximum(jnp.minimum(level, last) - wide, 0)

    def product(d, j):
        total = None
        for c in range(nx):
            term = jnp.dot(cot_t[:, c * half:(c + 1) * half],
                           mats[d, c, :, j * half:(j + 1) * half], preferred_element_type=F32)
            total = term if total is None else total + term
        return total

    @pl.when(is_col)
    def _():
        cot_t[...] = acc_col[...].astype(BF16)
        src_t[...] = cot_t[...]
        for d in range(2):
            for k in range(1, nx):
                gather_copy(d, k).wait_recv()

        @pl.when(level < last)
        def _():
            for d in (first, second):
                for j in range(nx):
                    wide_out[d, j] = product(d, j).astype(BF16)
                    wide_copy(j, wide_level, d, target_of(d)).start()

        @pl.when(is_last)
        def _():
            for j in range(nx):
                wide_out[0, j] = (product(0, j) + product(1, j)).astype(BF16)
                wide_copy(j, wide_level, 0, up_row(1 << last)).start()

        for k in range(1, nx):
            cot_copy(k).start()
        cot_half[own_cols, :] = cot_t[:, low_half]

        @pl.when(level == wide)
        def _():
            forward_near()

        for k in range(1, nx):
            cot_copy(k).wait_recv()
        factor_t[...] = cot_half[...]

    low_store = pltpu.make_async_copy(grad_v.at[0], low_out.at[0], store_sem.at[0])
    up_store = pltpu.make_async_copy(grad_v.at[1], up_out.at[0], store_sem.at[1])
    src_store = pltpu.make_async_copy(src_v, src_out.at[0], store_sem.at[2])

    @pl.when(is_root)
    def _():
        grad_v[...] = jnp.zeros_like(grad_v)

    @pl.when(jnp.logical_not(is_root))
    def _():
        factor[...] = -(factor_t[...].T)

        def act(d):
            for k in range(1, nx):
                near_copy(d, k).wait_recv()
        each_near(act)
        for d in range(2):
            which = d if d == 0 else jnp.where(is_last, 0, 1)
            full = jnp.concatenate([near[which, c] for c in range(nx)], axis=1)
            grad_v[d] = lax.dot_general(
                factor[...], full, (((1,), (1,)), ((), ())),
                preferred_element_type=F32).astype(BF16)

    low_store.start()
    up_store.start()

    @pl.when(is_half)
    def _():
        for k in range(1, nx):
            src_copy(k).wait_recv()

    src_v[...] = src_t[...].T
    src_store.start()

    each_sol(lambda c: c.wait_send())

    @pl.when(jnp.logical_not(is_root))
    def _():
        def act(d):
            for k in range(1, nx):
                near_copy(d, k).wait_send()
        each_near(act)
        for k in range(1, nx):
            cot_copy(k).wait_send()

    @pl.when(is_half)
    def _():
        for k in range(1, nx):
            src_copy(k).wait_send()
        for k in range(nx):
            col_copy(k, half_level, second, row).wait_send()

        @pl.when(level < wide - 1)
        def _():
            for k in range(nx):
                half_copy(k, 0, first, row).wait_send()

        @pl.when(level == wide - 1)
        def _():
            for k in range(nx):
                col_copy(k, half_level, first, row).wait_send()

    @pl.when(is_col)
    def _():
        for d in range(2):
            for k in range(1, nx):
                gather_copy(d, k).wait_send()
        for j in range(nx):
            wide_copy(j, wide_level, 0, row).wait_send()

            @pl.when(level < last)
            def _():
                wide_copy(j, wide_level, 1, row).wait_send()

    low_store.wait()
    up_store.wait()
    src_store.wait()


def body(n, nx, lower_coupling, upper_coupling, solution, cotangent):
    _, half, block = lower_coupling.shape
    width = cotangent.shape[2]
    full = width * nx
    levels = n.bit_length() - 1
    wide = min(2, levels - 1)
    dma = pltpu.SemaphoreType.DMA
    return pl.pallas_call(
        functools.partial(kernel, n, nx, wide),
        out_shape=(
            jax.ShapeDtypeStruct(cotangent.shape, BF16),
            jax.ShapeDtypeStruct(lower_coupling.shape, BF16),
            jax.ShapeDtypeStruct(upper_coupling.shape, BF16),
        ),
        in_specs=[pl.BlockSpec(memory_space=pl.ANY)] * 4,
        out_specs=[pl.BlockSpec(memory_space=pl.ANY)] * 3,
        scratch_shapes=[
            pltpu.VMEM((2, nx, half, block), BF16),
            pltpu.VMEM((block, width), BF16),
            pltpu.VMEM((block, width), BF16),
            pltpu.VMEM((width, block), BF16),
            pltpu.VMEM((full, half), BF16),
            pltpu.VMEM((full, half), F32),
            pltpu.VMEM((full, half), BF16),
            pltpu.VMEM((half, full), BF16),
            pltpu.VMEM((nx, full, half), BF16),
            pltpu.VMEM((max(wide - 1, 1), 2, nx, full, half), BF16),
            pltpu.VMEM((width, block), F32),
            pltpu.VMEM((2, nx, width, block), BF16),
            pltpu.VMEM((wide, 2, nx, width, block), BF16),
            pltpu.VMEM((2, nx, width, half), BF16),
            pltpu.VMEM((levels - wide, 2, nx, width, half), BF16),
            pltpu.VMEM((2, nx, block, width), BF16),
            pltpu.VMEM((width, block), BF16),
            pltpu.VMEM((block, width), BF16),
            pltpu.VMEM((2, half, block), BF16),
            dma((4,)), dma((3,)),
            dma((nx,)), dma((nx,)),
            dma((nx,)), dma((max(wide - 1, 1), 2, nx)),
            dma((2, nx)), dma((wide, 2, nx)),
            dma((2, nx)), dma((levels - wide, 2, nx)),
            dma((2, nx)), dma((2, nx)),
            dma((levels, 2)), dma((2,)),
            dma((2, nx)), dma((2, nx)),
            dma((nx,)), dma((nx,)),
        ],
        compiler_params=pltpu.CompilerParams(
            collective_id=0, has_side_effects=True, vmem_limit_bytes=62 * 1024 * 1024),
    )(lower_coupling, upper_coupling, solution, cotangent)


def solution(mesh):
    in_specs = (
        P("rows", "cols", None),
        P("rows", "cols", None),
        P("rows", None, "cols"),
        P("rows", None, "cols"),
    )
    out_specs = (P("rows", None, "cols"), P("rows", "cols", None), P("rows", "cols", None))
    local = functools.partial(body, mesh.shape["rows"], mesh.shape["cols"])
    return jax.shard_map(local, mesh=mesh, in_specs=in_specs, out_specs=out_specs, check_vma=False)
```

time: 67.1 us -> 58.7 us (0.87)
  Pallas kernels: 59.2 us -> 52.9 us
  local copies, waits for them, and re-layouts: 6.99 us -> 4.99 us
    pallas_call x1, Pallas kernels: 59.2 us -> 52.9 us  [body(): pl.pallas_call(functools.partial(kernel, n, nx, wide), out_shape=(jax.Sha...]
    unnamed x11 -> x5, local copies, waits for them, and re-layouts: 6.99 us -> 4.99 us
where the time goes in v2:
time: 58.7 us; the launch traced here: 58.5 us
  Pallas kernels  52.9 us (90%)
  local copies, waits for them, and re-layouts  4.99 us (9%)
  between operations  0.64 us (1%)
    pallas_call x1, Pallas kernels, body(): pl.pallas_call(functools.partial(kernel, n, nx, wide), out_shape=(jax.Sha...  52.9 us
    unnamed x5, local copies, waits for them, and re-layouts  4.99 us

profile of v2, /device:TPU:1, one launch (start us, length us, event | category | flops | bytes accessed | tf_op | source)
XLA Modules:
  0.0 58.5 jit_solution(14464884822304740840)
XLA Ops:
  0.6 52.9 %shard_map.67 = (bf16[1,1024,128]{2,1,0:T(8,128)(2,1)}, bf16[1,512,1024]{2,1,0:T(8,128)(2,1)}, bf16[1,512,1024]{2,1,0:T(8,128)(2,1)}) custom-call(bf16[1,512,1024]{2,1,0:T(8,128)(2,1)} %lower_hbm.1, bf16[1,512,1024]{2,1,0:T(8,128)(2,1)} %upper_hbm.1, bf16[1,1024,128]{2,1,0:T(8,128)(2,1)} %sol_hbm.1, bf16[1,1024,128]{2,1,0:T(8,128)(2,1)} %cot_hbm.1), custom_call_target="tpu_custom_call" | custom-call | tf_op jit(solution)/shard_map/pallas_call | solution.py:412
  53.5 1.7 %copy.10 = bf16[1,1024,128]{2,1,0:T(8,128)(2,1)} copy(bf16[1,1024,128]{2,1,0:T(8,128)(2,1)} %get-tuple-element.6) | data formatting | bytes 524288
  55.2 0.0 copy-start
  55.2 2.4 %copy.11 = bf16[1,512,1024]{2,1,0:T(8,128)(2,1)} copy(bf16[1,512,1024]{2,1,0:T(8,128)(2,1)} %get-tuple-element.7) | data formatting | bytes 2097152
  57.5 0.0 copy-done
  57.5 1.0 %copy.12 = bf16[1,512,1024]{2,1,0:T(8,128)(2,1)} copy(bf16[1,512,1024]{2,1,0:T(8,128)(2,1)S(1)} %copy-done) | data formatting | bytes 2097152
Async XLA Ops:
  55.2 2.4 %copy-start = (bf16[1,512,1024]{2,1,0:T(8,128)(2,1)S(1)}, bf16[1,512,1024]{2,1,0:T(8,128)(2,1)}, u32[]{:S(2)}) copy-start(bf16[1,512,1024]{2,1,0:T(8,128)(2,1)} %get-tuple-element.8) | copy-start | bytes 3145732

commit v3 on v2

--- a/solution.py
+++ b/solution.py
@@ -36,6 +36,10 @@
         stride = jnp.where(level > l, 2 << l, stride)
     stride = jnp.where(is_root, 0, stride)
 
+    span = jnp.maximum(stride, 1)
+    first = jnp.where(lax.rem(offset + span, 4 * span) == 2 * span, 0, 1)
+    second = 1 - first
+
     def other(k):
         return lax.rem(col + k, nx)
 
@@ -91,6 +95,13 @@
             send_sem=gat_ss.at[d, k], recv_sem=gat_rs.at[d, k],
             device_id=(row, other(k)), device_id_type=MESH)
 
+    def gather(which, act):
+        for d in range(2):
+            @pl.when(which == d)
+            def _():
+                for k in range(1, nx):
+                    act(gather_copy(d, k))
+
     @pl.when(is_half)
     def _():
         for k in range(1, nx):
@@ -98,9 +109,7 @@
 
     @pl.when(is_col)
     def _():
-        for d in range(2):
-            for k in range(1, nx):
-                gather_copy(d, k).start()
+        gather(first, lambda c: c.start())
 
     def sol_copy(l, d):
         target = up_row(1 << l) if d == 0 else down_row(1 << l)
@@ -173,9 +182,6 @@
             send_sem=src_ss.at[k], recv_sem=src_rs.at[k],
             device_id=(row, to), device_id_type=MESH)
 
-    span = jnp.maximum(stride, 1)
-    first = jnp.where(lax.rem(offset + span, 4 * span) == 2 * span, 0, 1)
-    second = 1 - first
 
     def target_of(d):
         return jnp.where(d == 0, up_row(stride), down_row(stride))
@@ -251,6 +257,10 @@
                     total = term if total is None else total + term
             acc_col[...] = acc_col[...] - total
             if l == 0:
+                @pl.when(is_col)
+                def _():
+                    gather(second, lambda c: c.start())
+
                 loads[3].wait()
                 send_sol()
         loads[1].wait()
@@ -294,19 +304,20 @@
     def _():
         cot_t[...] = acc_col[...].astype(BF16)
         src_t[...] = cot_t[...]
-        for d in range(2):
-            for k in range(1, nx):
-                gather_copy(d, k).wait_recv()
+        gather(first, lambda c: c.wait_recv())
 
         @pl.when(level < last)
         def _():
             for d in (first, second):
+                if d is second:
+                    gather(second, lambda c: c.wait_recv())
                 for j in range(nx):
                     wide_out[d, j] = product(d, j).astype(BF16)
                     wide_copy(j, wide_level, d, target_of(d)).start()
 
         @pl.when(is_last)
         def _():
+            gather(second, lambda c: c.wait_recv())
             for j in range(nx):
                 wide_out[0, j] = (product(0, j) + product(1, j)).astype(BF16)
                 wide_copy(j, wide_level, 0, up_row(1 << last)).start()

time: 58.7 us -> 56.8 us (0.968)
  Pallas kernels: 52.9 us -> 50.9 us
    pallas_call x1, Pallas kernels: 52.9 us -> 50.9 us  [body(): pl.pallas_call(functools.partial(kernel, n, nx, wide), out_shape=(jax.Sha...]
where the time goes in v3:
time: 56.8 us; the launch traced here: 56.6 us
  Pallas kernels  50.9 us (90%)
  local copies, waits for them, and re-layouts  4.99 us (9%)
  between operations  0.64 us (1%)
    pallas_call x1, Pallas kernels, body(): pl.pallas_call(functools.partial(kernel, n, nx, wide), out_shape=(jax.Sha...  50.9 us
    unnamed x5, local copies, waits for them, and re-layouts  4.99 us

profile of v3, /device:TPU:1, one launch (start us, length us, event | category | flops | bytes accessed | tf_op | source)
XLA Modules:
  0.0 56.6 jit_solution(9890073759097863128)
XLA Ops:
  0.6 50.9 %shard_map.67 = (bf16[1,1024,128]{2,1,0:T(8,128)(2,1)}, bf16[1,512,1024]{2,1,0:T(8,128)(2,1)}, bf16[1,512,1024]{2,1,0:T(8,128)(2,1)}) custom-call(bf16[1,512,1024]{2,1,0:T(8,128)(2,1)} %lower_hbm.1, bf16[1,512,1024]{2,1,0:T(8,128)(2,1)} %upper_hbm.1, bf16[1,1024,128]{2,1,0:T(8,128)(2,1)} %sol_hbm.1, bf16[1,1024,128]{2,1,0:T(8,128)(2,1)} %cot_hbm.1), custom_call_target="tpu_custom_call" | custom-call | tf_op jit(solution)/shard_map/pallas_call | solution.py:423
  51.6 1.7 %copy.10 = bf16[1,1024,128]{2,1,0:T(8,128)(2,1)} copy(bf16[1,1024,128]{2,1,0:T(8,128)(2,1)} %get-tuple-element.6) | data formatting | bytes 524288
  53.2 0.0 copy-start
  53.2 2.4 %copy.11 = bf16[1,512,1024]{2,1,0:T(8,128)(2,1)} copy(bf16[1,512,1024]{2,1,0:T(8,128)(2,1)} %get-tuple-element.7) | data formatting | bytes 2097152
  55.6 0.0 copy-done
  55.6 1.0 %copy.12 = bf16[1,512,1024]{2,1,0:T(8,128)(2,1)} copy(bf16[1,512,1024]{2,1,0:T(8,128)(2,1)S(1)} %copy-done) | data formatting | bytes 2097152
Async XLA Ops:
  53.2 2.4 %copy-start = (bf16[1,512,1024]{2,1,0:T(8,128)(2,1)S(1)}, bf16[1,512,1024]{2,1,0:T(8,128)(2,1)}, u32[]{:S(2)}) copy-start(bf16[1,512,1024]{2,1,0:T(8,128)(2,1)} %get-tuple-element.8) | copy-start | bytes 3145732

commit v4 on v3

--- a/solution.py
+++ b/solution.py
@@ -245,6 +245,15 @@
         send_sol()
         forward_near()
 
+    low_store = pltpu.make_async_copy(grad_v.at[0], low_out.at[0], store_sem.at[0])
+    up_store = pltpu.make_async_copy(grad_v.at[1], up_out.at[0], store_sem.at[1])
+
+    @pl.when(is_root)
+    def _():
+        grad_v[...] = jnp.zeros_like(grad_v)
+        low_store.start()
+        up_store.start()
+
     @pl.when(level >= wide)
     def _():
         acc_col[...] = cot_t[...].astype(F32)
@@ -334,13 +343,7 @@
             cot_copy(k).wait_recv()
         factor_t[...] = cot_half[...]
 
-    low_store = pltpu.make_async_copy(grad_v.at[0], low_out.at[0], store_sem.at[0])
-    up_store = pltpu.make_async_copy(grad_v.at[1], up_out.at[0], store_sem.at[1])
     src_store = pltpu.make_async_copy(src_v, src_out.at[0], store_sem.at[2])
-
-    @pl.when(is_root)
-    def _():
-        grad_v[...] = jnp.zeros_like(grad_v)
 
     @pl.when(jnp.logical_not(is_root))
     def _():
@@ -357,8 +360,8 @@
                 factor[...], full, (((1,), (1,)), ((), ())),
                 preferred_element_type=F32).astype(BF16)
 
-    low_store.start()
-    up_store.start()
+        low_store.start()
+        up_store.start()
 
     @pl.when(is_half)
     def _():

time: 56.8 us -> 56.3 us (level)
  Pallas kernels: 50.9 us -> 50.2 us
    pallas_call x1, Pallas kernels: 50.9 us -> 50.2 us  [body(): pl.pallas_call(functools.partial(kernel, n, nx, wide), out_shape=(jax.Sha...]
where the time goes in v4:
time: 56.3 us; the launch traced here: 55.9 us
  Pallas kernels  50.2 us (89%)
  local copies, waits for them, and re-layouts  4.99 us (9%)
  between operations  0.64 us (1%)
    pallas_call x1, Pallas kernels, body(): pl.pallas_call(functools.partial(kernel, n, nx, wide), out_shape=(jax.Sha...  50.2 us
    unnamed x5, local copies, waits for them, and re-layouts  4.99 us

profile of v4, /device:TPU:1, one launch (start us, length us, event | category | flops | bytes accessed | tf_op | source)
XLA Modules:
  0.0 55.9 jit_solution(16757402915331919564)
XLA Ops:
  0.6 50.2 %shard_map.67 = (bf16[1,1024,128]{2,1,0:T(8,128)(2,1)}, bf16[1,512,1024]{2,1,0:T(8,128)(2,1)}, bf16[1,512,1024]{2,1,0:T(8,128)(2,1)}) custom-call(bf16[1,512,1024]{2,1,0:T(8,128)(2,1)} %lower_hbm.1, bf16[1,512,1024]{2,1,0:T(8,128)(2,1)} %upper_hbm.1, bf16[1,1024,128]{2,1,0:T(8,128)(2,1)} %sol_hbm.1, bf16[1,1024,128]{2,1,0:T(8,128)(2,1)} %cot_hbm.1), custom_call_target="tpu_custom_call" | custom-call | tf_op jit(solution)/shard_map/pallas_call | solution.py:426
  50.9 1.7 %copy.10 = bf16[1,1024,128]{2,1,0:T(8,128)(2,1)} copy(bf16[1,1024,128]{2,1,0:T(8,128)(2,1)} %get-tuple-element.6) | data formatting | bytes 524288
  52.5 0.0 copy-start
  52.5 2.4 %copy.11 = bf16[1,512,1024]{2,1,0:T(8,128)(2,1)} copy(bf16[1,512,1024]{2,1,0:T(8,128)(2,1)} %get-tuple-element.7) | data formatting | bytes 2097152
  54.9 0.0 copy-done
  54.9 1.0 %copy.12 = bf16[1,512,1024]{2,1,0:T(8,128)(2,1)} copy(bf16[1,512,1024]{2,1,0:T(8,128)(2,1)S(1)} %copy-done) | data formatting | bytes 2097152
Async XLA Ops:
  52.5 2.4 %copy-start = (bf16[1,512,1024]{2,1,0:T(8,128)(2,1)S(1)}, bf16[1,512,1024]{2,1,0:T(8,128)(2,1)}, u32[]{:S(2)}) copy-start(bf16[1,512,1024]{2,1,0:T(8,128)(2,1)} %get-tuple-element.8) | copy-start | bytes 3145732
